TPU v7x, 512 devices: a whole 4x4x16 slice. The times are simulated.
512 devices in a mesh: seq: 64 (over x, z), head: 8 (over y, core).
Axes of the slice: x: 4, y: 4, z: 16, core: 2. Of those that a mesh axis runs over, the one named last changes fastest.
Arguments:
- q_raw: bfloat16 [8192, 4096], P('seq', 'head'), may hold values from -6 to 6
- k_raw: bfloat16 [8192, 4096], P('seq', 'head'), may hold values from -6 to 6
- v_raw: bfloat16 [8192, 4096], P('seq', 'head'), may hold values from -7.5 to 7.5
- log_decay: bfloat16 [8192, 4096], P('seq', 'head'), may hold values from -0.7 to 0
- beta_logit: float32 [32, 8192], P('head', 'seq'), may hold values from -8 to 5
- conv_weight: float32 [3, 4, 4096], P(None, None, 'head'), may hold values from -3 to 3
- norm_gain: float32 [4096], P('head'), may hold values from 0.1 to 1.9
- out_weight: bfloat16 [4096, 2304], P('head'), may hold values from -0.09375 to 0.09375
Outputs:
- layer_out: bfloat16 [8192, 2304], P(('seq', 'head'))
All inputs are finite; a program needn't handle non-finite values.
Results may differ from a plain program's by a relative error of at most 0.017.
Values may be sent and summed in bfloat16 or wider, within the bound.
A program may use at most 128 MiB of HBM per device.

v0:
```python
import jax
import jax.numpy as jnp
from jax import lax
from jax.sharding import PartitionSpec as P

HEAD_WIDTH = 128
CONV = 4
BLOCK = 64


highest = lax.Precision.HIGHEST


def shifted(shard, axis, by):
    count = lax.axis_size(axis)
    pairs = [(i, i + by) for i in range(count) if 0 <= i + by < count]
    return lax.ppermute(shard, axis, pairs)


def carried_in(shard, axis, combine, identity):
    count, position = (lax.axis_size(axis), lax.axis_index(axis))
    everything = jax.tree.map(lambda part: lax.all_gather(part, axis), shard)
    start = jax.tree.map(
        lambda part, zero: jnp.broadcast_to(jnp.asarray(zero, part.dtype), part.shape),
        shard,
        identity,
    )

    def hop(k, before):
        reached = k < position
        new = combine(before, jax.tree.map(lambda part: part[k], everything))
        return jax.tree.map(lambda a, b: jnp.where(reached, a, b), new, before)

    return lax.fori_loop(0, count, hop, start)


def contract_product(pattern, left, right):
    return jnp.einsum(pattern, left, right, precision=highest)


def unit_rows(values_in):
    return values_in * lax.rsqrt(jnp.sum(values_in * values_in, axis=-1, keepdims=True) + 1e-06)


def conv_block(padded, conv_taps):
    out_len = padded.shape[0] - conv_taps.shape[0] + 1
    widened = padded.astype(jnp.float32)
    summed = jnp.zeros((out_len, widened.shape[1]), jnp.float32)
    for offset in range(conv_taps.shape[0]):
        summed = summed + widened[offset : offset + out_len] * conv_taps[offset]
    return jax.nn.silu(summed)


def block_terms(queries, keys_in, values_in, log_rate, strength):
    block_len = queries.shape[-2]
    filled = jnp.ones((block_len, block_len), jnp.float32)
    inclusive = jnp.tril(filled)
    strict = jnp.tril(filled, -1)
    cumulative = jnp.einsum("ts,...sk->...tk", inclusive, log_rate, precision=highest)
    last_row = cumulative[..., -1:, :]
    key_pos = keys_in * jnp.exp(cumulative)
    key_neg = keys_in * jnp.exp(-cumulative)
    query_position = queries * jnp.exp(cumulative)
    key_final_decay = keys_in * jnp.exp(last_row - cumulative)
    lower = contract_product("...tk,...sk->...ts", key_pos, key_neg) * strict
    attention_scores = contract_product("...tk,...sk->...ts", query_position, key_neg) * inclusive
    system = jnp.eye(block_len, dtype=jnp.float32) + strength[..., :, None] * lower
    right_side = strength[..., :, None] * jnp.concatenate([key_pos, values_in], axis=-1)
    solved = jax.scipy.linalg.solve_triangular(system, right_side, lower=True, unit_diagonal=True)
    key_width = keys_in.shape[-1]
    return (
        query_position,
        key_final_decay,
        jnp.exp(last_row),
        solved[..., :key_width],
        solved[..., key_width:],
        attention_scores,
    )


def body(q_raw, k_raw, v_raw, log_decay, beta_logit, conv_weight, norm_gain, out_weight):
    tok_rows, feat_width = q_raw.shape
    local_heads = beta_logit.shape[0]
    block_count = tok_rows // BLOCK
    rim_len = CONV - 1
    stacked_rims = jnp.stack(
        [q_raw[tok_rows - rim_len :], k_raw[tok_rows - rim_len :], v_raw[tok_rows - rim_len :]]
    )
    rims_in = shifted(stacked_rims, "seq", 1)
    sources = (q_raw, k_raw, v_raw)
    convolved = [
        conv_block(jnp.concatenate([rims_in[which], sources[which]], axis=0), conv_weight[which])
        for which in range(3)
    ]

    def to_blocks(matrix):
        return matrix.reshape(block_count, BLOCK, local_heads, HEAD_WIDTH).transpose(0, 2, 1, 3)

    queries = unit_rows(to_blocks(convolved[0]))
    keys_in = unit_rows(to_blocks(convolved[1]))
    values_in = to_blocks(convolved[2])
    log_rate = to_blocks(log_decay.astype(jnp.float32))
    strength = (
        jax.nn.sigmoid(beta_logit).reshape(local_heads, block_count, BLOCK).transpose(1, 0, 2)
    )
    (
        query_position,
        key_final_decay,
        final_decay,
        resolved_keys,
        resolved_values,
        attention_scores,
    ) = block_terms(queries, keys_in, values_in, log_rate, strength)
    query_eff = query_position - contract_product(
        "...ts,...sk->...tk", attention_scores, resolved_keys
    )
    intra_out = contract_product("...ts,...sv->...tv", attention_scores, resolved_values)
    transit = jnp.eye(HEAD_WIDTH, dtype=jnp.float32) * jnp.swapaxes(
        final_decay, -1, -2
    ) - contract_product("...ck,...cj->...kj", key_final_decay, resolved_keys)
    injected = contract_product("...ck,...cv->...kv", key_final_decay, resolved_values)
    unit_maps = jnp.broadcast_to(
        jnp.eye(HEAD_WIDTH, dtype=jnp.float32), (local_heads, HEAD_WIDTH, HEAD_WIDTH)
    )
    empty = jnp.zeros((local_heads, HEAD_WIDTH, HEAD_WIDTH), jnp.float32)

    def compose(carried, inputs):
        product, memory_state = carried
        transition_matrix, injected_update = inputs
        product_next = contract_product("hkj,hjl->hkl", transition_matrix, product)
        next_memory_state = (
            contract_product("nrt,ntw->nrw", transition_matrix, memory_state) + injected_update
        )
        return ((product_next, next_memory_state), None)

    (product_end, memory_end), _ = lax.scan(compose, (unit_maps, empty), (transit, injected))

    def combine_pairs(earlier_tokens, later_tokens):
        return (
            contract_product("hkj,hjl->hkl", later_tokens[0], earlier_tokens[0]),
            contract_product("nrt,ntw->nrw", later_tokens[0], earlier_tokens[1]) + later_tokens[1],
        )

    prefix = carried_in((product_end, memory_end), "seq", combine_pairs, (unit_maps, empty))
    entering = prefix[1]

    def replay(memory_state, inputs):
        transition_matrix, injected_update, current_query = inputs
        carried_state_term = contract_product("xiy,xyp->xip", current_query, memory_state)
        return (
            contract_product("nrt,ntw->nrw", transition_matrix, memory_state) + injected_update,
            carried_state_term,
        )

    _, carried_out = lax.scan(replay, entering, (transit, injected, query_eff))
    attention_output = intra_out + carried_out
    gain = norm_gain.reshape(local_heads, 1, HEAD_WIDTH)
    normed = (
        attention_output
        * lax.rsqrt(jnp.mean(attention_output * attention_output, axis=-1, keepdims=True) + 1e-06)
        * gain
    )
    normed = normed.transpose(0, 2, 1, 3).reshape(tok_rows, feat_width).astype(jnp.bfloat16)
    return lax.psum_scatter(
        jnp.dot(normed, out_weight, preferred_element_type=jnp.float32).astype(jnp.bfloat16),
        "head",
        scatter_dimension=0,
        tiled=True,
    )


def solution(mesh):
    in_specs = (
        P("seq", "head"),
        P("seq", "head"),
        P("seq", "head"),
        P("seq", "head"),
        P("head", "seq"),
        P(None, None, "head"),
        P("head"),
        P("head", None),
    )
    out_specs = P(("seq", "head"), None)
    return jax.shard_map(body, mesh=mesh, in_specs=in_specs, out_specs=out_specs, check_vma=False)
```

profile of v0, /device:TPU:7, one launch (start us, length us, event | category | flops | bytes accessed | tf_op | source)
XLA Modules:
  0.0 612.3 jit_solution(6768217466483111294)
XLA Ops:
  8.1 3.5 collective-permute-start
  12.5 1.5 fusion.69
  16.3 4.2 collective-permute-done
  24.4 40.0 %custom-call.4 = f32[2,4,1,64,64]{3,4,2,1,0:T(8,128)} custom-call(f32[2,4,1,64,64]{4,3,2,1,0:T(8,128)S(1)} %fusion.30), custom_call_target="InvertDiagBlocksLowerTriangular" | custom-call | tf_op jit(solution)/shard_map/jit(_solve_triangular)/vmap(vmap())/triangular_solve | solution.py:69
  67.9 1.7 fusion.31
  70.8 2.2 convolution_subtract_fusion
  73.7 8.2 %while.40 = (s32[]{:T(128)}, f32[4,128,128]{2,1,0:T(8,128)}, f32[4,128,128]{2,1,0:T(8,128)}, f32[2,4,128,128]{3,2,1,0:T(8,128)S(1)}, f32[2,4,128,128]{3,2,1,0:T(8,128)S(1)}, /*index=5*/s32[]{:T(128)}, s32[]{:T(128)}) while((s32[]{:T(128)}, f32[4,128,128]{2,1,0:T(8,128)}, f32[4,128,128]{2,1,0:T(8,128)}, ...), condition=%wide.region_3.4_spmd.clone, body=%wide.region_2.3_spmd.clone.sunk | while | flops 201457664 | bytes 2884699 | solution.py:136
  85.8 1.8 convolution_multiply_fusion.1
  88.3 2.1 convolution_subtract_fusion.1
  90.4 182.6 %all-gather.5.cloned.1.call-done = f32[256,128,128]{2,1,0:T(8,128)} async-done(((f32[4,128,128]{2,1,0:T(8,128)}), f32[256,128,128]{2,1,0:T(8,128)}) %all-gather.5.cloned.1.call-update) | async-done | bytes 16777232 | tf_op jit(solution)/shard_map/all_gather | solution.py:22
  273.0 193.0 %all-gather.7.cloned.1.call-done = f32[256,128,128]{2,1,0:T(8,128)} async-done(((f32[4,128,128]{2,1,0:T(8,128)}), f32[256,128,128]{2,1,0:T(8,128)}) %all-gather.7.cloned.1.call-update) | async-done | bytes 16777232 | tf_op jit(solution)/shard_map/all_gather | solution.py:22
  466.0 94.9 %while.41 = (s32[]{:T(128)}, f32[4,128,128]{2,1,0:T(8,128)S(1)}, s32[]{:T(128)}, f32[64,4,128,128]{3,2,1,0:T(8,128)}, f32[64,4,128,128]{3,2,1,0:T(8,128)}, /*index=5*/s32[]{:T(128)}, s32[]{:T(128)}) while((s32[]{:T(128)}, f32[4,128,128]{2,1,0:T(8,128)S(1)}, s32[]{:T(128)}, f32[64,4,128,128]{3,2,1,0:T(8,128)}, ...), condition=%wide.region_5.6_spmd.clone, body=%wide.region_4.5_spmd.clone.sunk | while | flops 100925440 | bytes 1837663 | solution.py:34
  466.0 1.4 fusion.102
  471.9 1.4 fusion.102
  473.4 1.4 fusion.102
  476.4 1.4 fusion.102
  483.8 1.4 fusion.102
  491.2 1.4 fusion.102
  498.6 1.4 fusion.102
  506.1 1.4 fusion.102
  513.5 1.4 fusion.102
  520.9 1.4 fusion.102
  528.3 1.4 fusion.102
  535.7 1.4 fusion.102
  543.1 1.4 fusion.102
  550.6 1.4 fusion.102
  558.0 1.4 fusion.102
  560.9 6.6 %while.39 = (s32[]{:T(128)}, f32[4,128,128]{2,1,0:T(8,128)S(1)}, f32[2,4,64,128]{3,2,1,0:T(8,128)}, f32[2,4,128,128]{3,2,1,0:T(8,128)S(1)}, f32[2,4,128,128]{3,2...) while((s32[]{:T(128)}, f32[4,128,128]{2,1,0:T(8,128)S(1)}, f32[2,4,64,128]{3,2,1,0:T(8,128)}, ...), condition=%wide.region_7.8_spmd, body=%wide.region_6.7_spmd.sunk | while | flops 151060480 | bytes 2099277 | solution.py:155
  561.0 1.9 fusion.94
  564.3 1.9 fusion.94
  567.6 1.5 multiply_reduce_fusion
  570.7 35.0 %reduce-scatter.2.cloned.1.call-done = bf16[16,2304]{1,0:T(8,128)(2,1)} async-done(((bf16[128,2304]{1,0:T(8,128)(2,1)}), bf16[16,2304]{1,0:T(8,128)(2,1)}) %reduce-scatter.2.cloned.1.call-update) | async-done | bytes 73744 | tf_op jit(solution)/shard_map/reduce_scatter | solution.py:164
  (197 shorter events, 101.9 us)
Async XLA Ops:
  6.5 562.8 %copy-start = (bf16[512,2304]{1,0:T(8,128)(2,1)S(1)}, bf16[512,2304]{1,0:T(8,128)(2,1)}, u32[]{:S(2)}) copy-start(bf16[512,2304]{1,0:T(8,128)(2,1)} %param.21) | copy-start | bytes 7077892
  6.5 266.4 %all-gather.5.cloned.1.call-start = ((), (), s32[]{:S(2)}) async-start(), calls=%async_computation.2 | async-start | bytes 17039360 | tf_op jit(solution)/shard_map/all_gather | solution.py:22
  8.1 12.5 %collective-permute-start = (bf16[3,3,512]{2,1,0:T(4,128)(2,1)S(1)}, bf16[3,3,512]{2,1,0:T(4,128)(2,1)S(1)}, u32[]{:S(2)}, u32[]{:S(2)}) collective-permute-start(bf16[3,3,512]{2,1,0:T(4,128)(2,1)S(1)} %pad_maximum_fusion), channel_id=1, source_target_pairs={{0,8},{8,16},{16,24},{24,32},{32,40},{40,48},{48,56},{56,64},{64,7... | collective-permute-start | bytes 27656 | tf_op jit(solution)/shard_map/ppermute | solution.py:17
  22.4 48.3 %copy-start.3 = (f32[2,64,4,128]{3,2,1,0:T(4,128)}, f32[2,64,4,128]{3,2,1,0:T(4,128)S(1)}, u32[]{:S(2)}) copy-start(f32[2,64,4,128]{3,2,1,0:T(4,128)S(1)} %reshape.114) | copy-start | bytes 786436
  22.9 47.9 %copy-start.2 = (f32[2,4,64,128]{3,2,1,0:T(8,128)}, f32[2,4,64,128]{3,2,1,0:T(8,128)S(1)}, u32[]{:S(2)}) copy-start(f32[2,4,64,128]{3,2,1,0:T(8,128)S(1)} %get-tuple-element.249) | copy-start | bytes 786436
  24.3 58.4 %copy-start.7 = (bf16[3,512]{1,0:T(4,128)(2,1)S(1)}, bf16[3,512]{1,0:T(4,128)(2,1)}, u32[]{:S(2)}) copy-start(bf16[3,512]{1,0:T(4,128)(2,1)} %get-tuple-element.245) | copy-start | bytes 9220
  24.3 59.4 %copy-start.8 = (f32[1,1,512]{2,1,0:T(1,128)S(1)}, f32[1,1,512]{2,1,0:T(1,128)}, u32[]{:S(2)}) copy-start(f32[1,1,512]{2,1,0:T(1,128)} %get-tuple-element.233) | copy-start | bytes 6148
  24.4 59.4 %copy-start.9 = (f32[1,1,512]{2,1,0:T(1,128)S(1)}, f32[1,1,512]{2,1,0:T(1,128)}, u32[]{:S(2)}) copy-start(f32[1,1,512]{2,1,0:T(1,128)} %get-tuple-element.240) | copy-start | bytes 6148
  24.4 59.4 %copy-start.10 = (f32[1,1,512]{2,1,0:T(1,128)S(1)}, f32[1,1,512]{2,1,0:T(1,128)}, u32[]{:S(2)}) copy-start(f32[1,1,512]{2,1,0:T(1,128)} %get-tuple-element.241) | copy-start | bytes 6148
  24.4 59.4 %copy-start.11 = (f32[1,1,512]{2,1,0:T(1,128)S(1)}, f32[1,1,512]{2,1,0:T(1,128)}, u32[]{:S(2)}) copy-start(f32[1,1,512]{2,1,0:T(1,128)} %get-tuple-element.242) | copy-start | bytes 6148
  69.6 1.1 copy-start.4
  73.7 495.4 %copy-start.12 = (f32[512]{0:T(512)S(1)}, f32[512]{0:T(512)}, u32[]{:S(2)}) copy-start(f32[512]{0:T(512)} %param.20) | copy-start | bytes 6148
  81.9 0.8 copy-start.1
  81.9 384.1 %all-gather.7.cloned.1.call-start = ((), (), s32[]{:S(2)}) async-start(), calls=%async_computation.3 | async-start | bytes 17039360 | tf_op jit(solution)/shard_map/all_gather | solution.py:22
  82.6 523.1 %reduce-scatter.2.cloned.1.call-start = ((), (), s32[]{:S(2)}) async-start(), calls=%async_computation.1 | async-start | bytes 663552 | tf_op jit(solution)/shard_map/reduce_scatter | solution.py:164
  87.6 0.7 copy-start.5
  90.4 477.2 %copy-start.6 = (f32[2,4,64,64]{3,2,1,0:T(8,128)S(1)}, f32[2,4,64,64]{3,2,1,0:T(8,128)}, u32[]{:S(2)}) copy-start(f32[2,4,64,64]{3,2,1,0:T(8,128)} %copy-done.5) | copy-start | bytes 393220
Sparse Core Ops, SparseCore 0:
  82.0 190.9 all-gather.4
  275.9 190.0 all-gather.6
  570.8 34.8 reduce-scatter.1
where the time goes:
time: 617 us; the launch traced here: 612 us
  waiting for transfers between devices  416 us (67%)
  matrix products  116 us (19%)
  other arithmetic  47.2 us (8%)
  local copies, waits for them, and re-layouts  14.2 us (2%)
  between operations  13.5 us (2%)
    all_gather x2, waiting for transfers between devices, carried_in(): everything = jax.tree.map(lambda part: lax.all_gather(part, axis), shard)  376 us
    dot_general x78, matrix products, contract_product(): return jnp.einsum(pattern, left, right, precision=highest)  112 us
    another operation x4, other arithmetic, block_terms(): jax.scipy.linalg.solve_triangular(system, right_side, lower=True, unit_di...  41.3 us
    reduce_scatter x1, waiting for transfers between devices, body(): lax.psum_scatter(jnp.dot(normed, out_weight, preferred_element_type=jnp.f...  35 us
  transfers between devices with their start and end apart: 4, of which 4 were waited for; matrix products, arithmetic and copies ran while one was open for 2% of the time, Pallas kernels for 0%

commit v1 on v0

v1 whole, which is shorter than its diff:
```python
import functools

import jax
import jax.numpy as jnp
from jax import lax
from jax.experimental import pallas as pl
from jax.experimental.pallas import tpu as pltpu
from jax.sharding import PartitionSpec as P

MESH = pl.DeviceIdType.MESH
F32 = jnp.float32
BF16 = jnp.bfloat16
HW = 128
CONV = 4
RIM = 16
CHUNKS = 3


def halves(value):
    high = value.astype(BF16)
    return high, (value - high.astype(F32)).astype(BF16)


def mm(a, b):
    return jnp.dot(a, b, preferred_element_type=F32)


def mm_full(a, b):
    a_hi, a_lo = halves(a)
    b_hi, b_lo = halves(b)
    wide = mm(jnp.concatenate([a_hi, a_lo], axis=1), jnp.concatenate([b_hi, b_hi], axis=0))
    return wide + mm(a_hi, b_lo)


def mm_exact_left(a_bf, b):
    b_hi, b_lo = halves(b)
    return mm(jnp.concatenate([a_bf, a_bf], axis=1), jnp.concatenate([b_hi, b_lo], axis=0))


def iotas(n):
    return lax.broadcasted_iota(jnp.int32, (n, n), 0), lax.broadcasted_iota(jnp.int32, (n, n), 1)


def unit_lower_inverses(lowers, row, col):
    differ = jnp.bitwise_xor(row, col)
    eye = (row == col).astype(F32)
    invs = [eye - jnp.where(differ == 1, low, 0.0) for low in lowers]
    level = 1
    while (2 << level) <= lowers[0].shape[0]:
        pick = lax.shift_right_logical(differ, level) == 1
        mids = [mm_full(jnp.where(pick, low, 0.0), inv) for low, inv in zip(lowers, invs)]
        invs = [inv - mm_full(inv, mid) for inv, mid in zip(invs, mids)]
        level += 1
    return invs


def compose(later_bf, earlier):
    width = earlier.shape[0]
    return earlier + mm_exact_left(later_bf[:, :width], earlier) + later_bf.astype(F32)


def kernel(
    q_hbm, k_hbm, v_hbm, ld_hbm, beta_hbm, taps_hbm, gain_hbm, w_hbm,
    o_ref,
    q_in, k_in, v_in, ld_in, beta_in, taps_in, gain_in, w_in,
    rims, ext, qeff, intra,
    e1_send, e1_recv, e2_send, e2_recv, e3_send, e3_recv, s4_send, s4_recv,
    parts, landed,
    local_sem, rim_send, rim_recv,
    l1s, l1r, l2s, l2r, l3s, l3r, l4s, l4r, rss, rsr,
):
    seq, head = lax.axis_index("seq"), lax.axis_index("head")
    seqs, heads = 64, 8
    x, a, b = seq // 16, (seq // 4) % 4, seq % 4
    toks, feat = q_in.shape
    local_heads = feat // HW

    sources = (q_hbm, k_hbm, v_hbm, ld_hbm, beta_hbm, taps_hbm, gain_hbm, w_hbm)
    inside = (q_in, k_in, v_in, ld_in, beta_in, taps_in, gain_in, w_in)
    loads = [
        pltpu.make_async_copy(src, dst, local_sem.at[i])
        for i, (src, dst) in enumerate(zip(sources, inside))
    ]
    for load in loads:
        load.start()

    def at1(d):
        return seq - b + (b + d) % 4

    def at2(d):
        return seq - 4 * a + 4 * ((a + d) % 4)

    def at3(d):
        return seq - 16 * x + 16 * ((x + d) % 4)

    after, before = (seq + 1) % seqs, (seq + seqs - 1) % seqs
    barrier = pltpu.get_barrier_semaphore()
    greet = [(after, head), (before, head)]
    greet += [(at(d), head) for at in (at1, at2, at3) for d in (1, 2, 3)]
    greet += [(seq, (head + d) % heads) for d in range(1, heads)]
    for device in greet:
        pl.semaphore_signal(barrier, inc=1, device_id=device, device_id_type=MESH)
    pl.semaphore_wait(barrier, len(greet))

    def remote(src, dst, send, recv, device):
        return pltpu.make_async_remote_copy(
            src_ref=src, dst_ref=dst, send_sem=send, recv_sem=recv, device_id=device, device_id_type=MESH
        )

    rim_copies = [
        remote(src.at[pl.ds(toks - RIM, RIM), :], rims.at[i], rim_send.at[i], rim_recv.at[i], (after, head))
        for i, src in enumerate((q_hbm, k_hbm, v_hbm))
    ]
    for copy in rim_copies:
        copy.start()

    row, col = iotas(toks)
    inclusive = row >= col
    strict = row > col
    eye = (row == col).astype(F32)
    for load in loads[3:7]:
        load.wait()
    cum = mm(inclusive.astype(BF16), ld_in[...])
    middle = cum[toks // 2 - 1 : toks // 2, :]
    last = cum[toks - 1 : toks, :]
    grow = jnp.exp(cum - middle)
    shrink = jnp.exp(middle - cum)
    from_start = jnp.exp(middle)
    to_end = jnp.exp(last - middle)
    loss = jnp.exp(last) - 1.0
    strength = 1.0 / (1.0 + jnp.exp(-beta_in[...]))

    conved = []
    for load in loads[:3]:
        load.wait()
    for copy in rim_copies:
        copy.wait_recv()
    for i, inp in enumerate((q_in, k_in, v_in)):
        ext[i, 0:RIM, :] = jnp.where(seq > 0, rims[i].astype(F32), 0.0)
        ext[i, RIM : RIM + toks, :] = inp[...].astype(F32)
        total = jnp.zeros((toks, feat), F32)
        for j in range(CONV):
            first = RIM - (CONV - 1) + j
            total = total + ext[i, first : first + toks, :] * taps_in[i, j : j + 1, :]
        conved.append(total / (1.0 + jnp.exp(-total)))

    queries, keys, values, lowers, scores, betas = [], [], [], [], [], []
    for h in range(local_heads):
        cols = slice(h * HW, (h + 1) * HW)
        q_h, k_h, v_h = (part[:, cols] for part in conved)
        q_h = q_h * lax.rsqrt(jnp.sum(q_h * q_h, axis=-1, keepdims=True) + 1e-06)
        k_h = k_h * lax.rsqrt(jnp.sum(k_h * k_h, axis=-1, keepdims=True) + 1e-06)
        beta = jnp.transpose(jnp.broadcast_to(strength[h : h + 1, :], (HW, toks)))
        key_pos, key_neg, query_pos = k_h * grow[:, cols], k_h * shrink[:, cols], q_h * grow[:, cols]
        both = mm_full(jnp.concatenate([key_pos, query_pos], axis=0), jnp.transpose(key_neg))
        lowers.append(jnp.where(strict, both[:toks] * beta, 0.0))
        scores.append(jnp.where(inclusive, both[toks:], 0.0))
        queries.append(query_pos * from_start[:, cols])
        keys.append(jnp.transpose(key_neg * to_end[:, cols]))
        values.append(jnp.concatenate([key_pos * from_start[:, cols] * beta, v_h * beta], axis=1))
    inverses = unit_lower_inverses(lowers, row, col)
    solved = [mm_full(inv, rhs) for inv, rhs in zip(inverses, values)]
    for h in range(local_heads):
        cols = slice(h * HW, (h + 1) * HW)
        outs = mm_full(jnp.concatenate([scores[h], keys[h]], axis=0), solved[h])
        qeff[h] = queries[h] - outs[:toks, :HW]
        intra[h] = outs[:toks, HW:]
        e1_send[h, :, :HW] = (eye * loss[:, cols] - outs[toks:, :HW]).astype(BF16)
        e1_send[h, :, HW:] = outs[toks:, HW:].astype(BF16)

    def exchange(send_of, recv, mine, at, sends, recvs):
        out, arrive = [], []
        for d in (1, 2, 3):
            copy = remote(send_of((mine + d) % 4), recv.at[mine], sends.at[d - 1], recvs.at[d - 1], (at(d), head))
            copy.start()
            out.append(copy)
            slot = (mine + 4 - d) % 4
            arrive.append(remote(send_of(slot), recv.at[slot], sends.at[d - 1], recvs.at[d - 1], (at(d), head)))
        return out, arrive

    out1, arrive1 = exchange(lambda h: e1_send.at[h], e1_recv, b, at1, l1s, l1r)
    e1_recv[b] = e1_send[b]
    for copy in arrive1:
        copy.wait_recv()
    maps1 = [e1_recv[0].astype(F32)]
    for n in (1, 2, 3):
        maps1.append(compose(e1_recv[n], maps1[-1]))

    e2_send[...] = maps1[3].astype(BF16)
    out2, arrive2 = exchange(lambda h: e2_send, e2_recv, a, at2, l2s, l2r)
    e2_recv[a] = e2_send[...]
    for copy in arrive2:
        copy.wait_recv()
    run = e2_recv[0].astype(F32)
    before2 = jnp.zeros_like(run)
    for n in (1, 2, 3):
        before2 = jnp.where(a == n, run, before2)
        run = compose(e2_recv[n], run)

    e3_send[...] = run.astype(BF16)
    out3, arrive3 = exchange(lambda h: e3_send, e3_recv, x, at3, l3s, l3r)
    for copy in arrive3:
        copy.wait_recv()
    state = e3_recv[0, :, HW:].astype(F32)
    entering = jnp.zeros_like(state)
    entering = jnp.where(x == 1, state, entering)
    for n in (1, 2):
        state = state + mm_exact_left(e3_recv[n, :, :HW], state) + e3_recv[n, :, HW:].astype(F32)
        entering = jnp.where(x == n + 1, state, entering)
    entering = entering + mm_full(before2[:, :HW], entering) + before2[:, HW:]
    s4_send[0] = entering.astype(BF16)
    for n in (1, 2, 3):
        s4_send[n] = (entering + mm_full(maps1[n - 1][:, :HW], entering) + maps1[n - 1][:, HW:]).astype(BF16)

    out4, arrive4 = exchange(lambda h: s4_send.at[h], s4_recv, b, at1, l4s, l4r)
    s4_recv[b] = s4_send[b]
    for copy in arrive4:
        copy.wait_recv()
    normed = []
    for h in range(local_heads):
        q_hi, q_lo = halves(qeff[h])
        state_h = s4_recv[h]
        attended = intra[h] + mm(
            jnp.concatenate([q_hi, q_lo], axis=1), jnp.concatenate([state_h, state_h], axis=0)
        )
        scale = lax.rsqrt(jnp.mean(attended * attended, axis=-1, keepdims=True) + 1e-06)
        normed.append((attended * scale * gain_in[:, h * HW : (h + 1) * HW]).astype(BF16))
    normed = jnp.concatenate(normed, axis=1)

    loads[7].wait()
    width = w_in.shape[1] // CHUNKS
    rows = toks // heads
    sent, coming = [], []
    for c in range(CHUNKS):
        cols = slice(c * width, (c + 1) * width)
        partial = mm(normed, w_in[:, cols]).astype(BF16)
        for t in range(heads):
            parts[t, :, cols] = partial[t * rows : (t + 1) * rows]
        for d in range(1, heads):
            to, source = (head + d) % heads, (head + heads - d) % heads
            at = pl.ds(c * width, width)
            copy = remote(
                parts.at[to, :, at], landed.at[head, :, at], rss.at[c, d - 1], rsr.at[c, d - 1], (seq, to)
            )
            copy.start()
            sent.append(copy)
            coming.append(
                remote(
                    parts.at[to, :, at], landed.at[source, :, at], rss.at[c, d - 1], rsr.at[c, d - 1], (seq, to)
                )
            )
    for c in range(CHUNKS):
        cols = slice(c * width, (c + 1) * width)
        summed = parts[head, :, cols].astype(F32)
        for d in range(1, heads):
            coming[c * (heads - 1) + d - 1].wait_recv()
            summed = summed + landed[(head + heads - d) % heads, :, cols].astype(F32)
        o_ref[:, cols] = summed.astype(BF16)
    for copy in rim_copies + out1 + out2 + out3 + out4 + sent:
        copy.wait_send()


def body(q_raw, k_raw, v_raw, log_decay, beta_logit, conv_weight, norm_gain, out_weight):
    toks, feat = q_raw.shape
    local_heads = feat // HW
    heads = lax.axis_size("head")
    width = out_weight.shape[1]
    dma = pltpu.SemaphoreType.DMA
    gain = norm_gain.reshape(1, feat)
    operands = (q_raw, k_raw, v_raw, log_decay, beta_logit, conv_weight, gain, out_weight)
    scratch = [pltpu.VMEM(op.shape, op.dtype) for op in operands]
    scratch += [
        pltpu.VMEM((3, RIM, feat), BF16),
        pltpu.VMEM((3, RIM + toks, feat), F32),
        pltpu.VMEM((local_heads, toks, HW), F32),
        pltpu.VMEM((local_heads, toks, HW), F32),
        pltpu.VMEM((4, HW, 2 * HW), BF16),
        pltpu.VMEM((4, HW, 2 * HW), BF16),
        pltpu.VMEM((HW, 2 * HW), BF16),
        pltpu.VMEM((4, HW, 2 * HW), BF16),
        pltpu.VMEM((HW, 2 * HW), BF16),
        pltpu.VMEM((4, HW, 2 * HW), BF16),
        pltpu.VMEM((4, HW, HW), BF16),
        pltpu.VMEM((4, HW, HW), BF16),
        pltpu.VMEM((heads, toks // heads, width), BF16),
        pltpu.VMEM((heads, toks // heads, width), BF16),
        dma((len(operands),)), dma((3,)), dma((3,)),
        dma((3,)), dma((3,)), dma((3,)), dma((3,)), dma((3,)), dma((3,)), dma((3,)), dma((3,)),
        dma((CHUNKS, heads - 1)), dma((CHUNKS, heads - 1)),
    ]
    return pl.pallas_call(
        kernel,
        out_shape=jax.ShapeDtypeStruct((toks // heads, width), BF16),
        in_specs=[pl.BlockSpec(memory_space=pl.ANY)] * len(operands),
        out_specs=pl.BlockSpec(memory_space=pltpu.VMEM),
        scratch_shapes=scratch,
        compiler_params=pltpu.CompilerParams(
            collective_id=0, has_side_effects=True, vmem_limit_bytes=48 * 2**20
        ),
        cost_estimate=pl.CostEstimate(flops=2 * 10**9, bytes_accessed=3 * 10**6, transcendentals=10**6),
    )(*operands)


def solution(mesh):
    in_specs = (
        P("seq", "head"),
        P("seq", "head"),
        P("seq", "head"),
        P("seq", "head"),
        P("head", "seq"),
        P(None, None, "head"),
        P("head"),
        P("head", None),
    )
    out_specs = P(("seq", "head"), None)
    return jax.shard_map(body, mesh=mesh, in_specs=in_specs, out_specs=out_specs, check_vma=False)
```

time: 617 us -> 71.6 us (0.12)
  the two profiles are of different devices: /device:TPU:7 before, /device:TPU:1 now
where the time goes in v1:
time: 71.6 us; the launch traced here: 71.3 us
  Pallas kernels  63.2 us (88%)
  local copies, waits for them, and re-layouts  8.01 us (11%)
    pallas_call x1, Pallas kernels, body(): pl.pallas_call(kernel, out_shape=jax.ShapeDtypeStruct((toks // heads, wid...  63.2 us
    unnamed x17, local copies, waits for them, and re-layouts  8.01 us

profile of v1, /device:TPU:1, one launch (start us, length us, event | category | flops | bytes accessed | tf_op | source)
XLA Modules:
  0.0 71.3 jit_solution(15082659469191950414)
XLA Ops:
  0.0 0.0 copy-start
  0.0 1.7 %copy-done = bf16[512,2304]{1,0:T(8,128)(2,1)S(1)} copy-done((bf16[512,2304]{1,0:T(8,128)(2,1)S(1)}, bf16[512,2304]{1,0:T(8,128)(2,1)}, u32[]{:S(2)}) %copy-start) | copy-done | bytes 2359320
  1.7 0.0 copy-start.1
  1.7 0.9 %copy-done.1 = bf16[128,512]{1,0:T(8,128)(2,1)S(1)} copy-done((bf16[128,512]{1,0:T(8,128)(2,1)S(1)}, bf16[128,512]{1,0:T(8,128)(2,1)}, u32[]{:S(2)}) %copy-start.1) | copy-done | bytes 131096
  2.6 0.0 copy-start.2
  2.6 0.9 %copy-done.2 = bf16[128,512]{1,0:T(8,128)(2,1)S(1)} copy-done((bf16[128,512]{1,0:T(8,128)(2,1)S(1)}, bf16[128,512]{1,0:T(8,128)(2,1)}, u32[]{:S(2)}) %copy-start.2) | copy-done | bytes 131096
  3.5 0.0 copy-start.3
  3.5 0.9 %copy-done.3 = bf16[128,512]{1,0:T(8,128)(2,1)S(1)} copy-done((bf16[128,512]{1,0:T(8,128)(2,1)S(1)}, bf16[128,512]{1,0:T(8,128)(2,1)}, u32[]{:S(2)}) %copy-start.3) | copy-done | bytes 131096
  4.4 0.0 copy-start.4
  4.4 0.9 %copy-done.4 = bf16[128,512]{1,0:T(8,128)(2,1)S(1)} copy-done((bf16[128,512]{1,0:T(8,128)(2,1)S(1)}, bf16[128,512]{1,0:T(8,128)(2,1)}, u32[]{:S(2)}) %copy-start.4) | copy-done | bytes 131096
  5.3 0.0 copy-start.5
  5.3 0.7 %copy-done.5 = f32[3,4,512]{2,1,0:T(4,128)S(1)} copy-done((f32[3,4,512]{2,1,0:T(4,128)S(1)}, f32[3,4,512]{2,1,0:T(4,128)}, u32[]{:S(2)}) %copy-start.5) | copy-done | bytes 24600
  6.0 0.0 copy-start.6
  6.0 0.7 copy-done.6
  6.7 0.0 copy-start.7
  6.7 0.7 copy-done.7
  7.4 63.2 %shard_map.82 = bf16[16,2304]{1,0:T(8,128)(2,1)S(1)} custom-call(bf16[128,512]{1,0:T(8,128)(2,1)S(1)} %copy-done.1, bf16[128,512]{1,0:T(8,128)(2,1)S(1)} %copy-done.2, bf16[128,512]{1,0:T(8,128)(2,1)S(1)} %copy-done.3, bf16[128,512]{1,0:T(8,128)(2,1)S(1)} %copy-done.4, f32[4,128]{1,0:T(4,128)S(1)} %copy-done.6, f32[3,4,512]{2,1,0:T(4,128)S(1)} %copy-done.5, ...), custom_call_target="tpu_custom_call" | custom-call | flops 2000000000 | bytes 3000000 | tf_op jit(solution)/shard_map/pallas_call | solution.py:291
  70.6 0.6 copy.10
Async XLA Ops:
  0.0 1.7 %copy-start = (bf16[512,2304]{1,0:T(8,128)(2,1)S(1)}, bf16[512,2304]{1,0:T(8,128)(2,1)}, u32[]{:S(2)}) copy-start(bf16[512,2304]{1,0:T(8,128)(2,1)} %w_hbm.1) | copy-start | bytes 7077892
  1.7 0.9 %copy-start.1 = (bf16[128,512]{1,0:T(8,128)(2,1)S(1)}, bf16[128,512]{1,0:T(8,128)(2,1)}, u32[]{:S(2)}) copy-start(bf16[128,512]{1,0:T(8,128)(2,1)} %q_hbm.1) | copy-start | bytes 393220
  2.6 0.9 %copy-start.2 = (bf16[128,512]{1,0:T(8,128)(2,1)S(1)}, bf16[128,512]{1,0:T(8,128)(2,1)}, u32[]{:S(2)}) copy-start(bf16[128,512]{1,0:T(8,128)(2,1)} %k_hbm.1) | copy-start | bytes 393220
  3.5 0.9 %copy-start.3 = (bf16[128,512]{1,0:T(8,128)(2,1)S(1)}, bf16[128,512]{1,0:T(8,128)(2,1)}, u32[]{:S(2)}) copy-start(bf16[128,512]{1,0:T(8,128)(2,1)} %v_hbm.1) | copy-start | bytes 393220
  4.4 0.9 %copy-start.4 = (bf16[128,512]{1,0:T(8,128)(2,1)S(1)}, bf16[128,512]{1,0:T(8,128)(2,1)}, u32[]{:S(2)}) copy-start(bf16[128,512]{1,0:T(8,128)(2,1)} %ld_hbm.1) | copy-start | bytes 393220
  5.3 0.7 %copy-start.5 = (f32[3,4,512]{2,1,0:T(4,128)S(1)}, f32[3,4,512]{2,1,0:T(4,128)}, u32[]{:S(2)}) copy-start(f32[3,4,512]{2,1,0:T(4,128)} %taps_hbm.1) | copy-start | bytes 73732
  6.0 0.7 copy-start.6
  6.7 0.7 copy-start.7

commit v2 on v1

--- a/solution.py
+++ b/solution.py
@@ -13,6 +13,7 @@
 HW = 128
 CONV = 4
 RIM = 16
+EDGE = 8
 CHUNKS = 3
 
 
@@ -54,6 +55,14 @@
     return invs
 
 
+def conv_silu(ext, taps, i, rows):
+    total = jnp.zeros((rows, ext.shape[2]), F32)
+    for j in range(CONV):
+        first = RIM - (CONV - 1) + j
+        total = total + ext[i, first : first + rows, :] * taps[i, j : j + 1, :]
+    return total / (1.0 + jnp.exp(-total))
+
+
 def compose(later_bf, earlier):
     width = earlier.shape[0]
     return earlier + mm_exact_left(later_bf[:, :width], earlier) + later_bf.astype(F32)
@@ -64,10 +73,10 @@
     o_ref,
     q_in, k_in, v_in, ld_in, beta_in, taps_in, gain_in, w_in,
     rims, ext, qeff, intra,
-    e1_send, e1_recv, e2_send, e2_recv, e3_send, e3_recv, s4_send, s4_recv,
-    parts, landed,
+    e1_send, e1_recv, e2_send, e2_recv, n3_send, n3_recv, e3_send, e3_recv, s4_send, s4_recv,
+    parts, paired, summed, landed,
     local_sem, rim_send, rim_recv,
-    l1s, l1r, l2s, l2r, l3s, l3r, l4s, l4r, rss, rsr,
+    l1s, l1r, l2s, l2r, l3s, l3r, l4s, l4r, prs, prr, rss, rsr,
 ):
     seq, head = lax.axis_index("seq"), lax.axis_index("head")
     seqs, heads = 64, 8
@@ -84,6 +93,11 @@
     for load in loads:
         load.start()
 
+    other = head + 1 - 2 * (head % 2)
+
+    def across(d):
+        return (head + 2 * d) % heads
+
     def at1(d):
         return seq - b + (b + d) % 4
 
@@ -97,22 +111,14 @@
     barrier = pltpu.get_barrier_semaphore()
     greet = [(after, head), (before, head)]
     greet += [(at(d), head) for at in (at1, at2, at3) for d in (1, 2, 3)]
-    greet += [(seq, (head + d) % heads) for d in range(1, heads)]
+    greet += [(seq, other)] + [(seq, across(d)) for d in (1, 2, 3)]
     for device in greet:
         pl.semaphore_signal(barrier, inc=1, device_id=device, device_id_type=MESH)
-    pl.semaphore_wait(barrier, len(greet))
 
     def remote(src, dst, send, recv, device):
         return pltpu.make_async_remote_copy(
             src_ref=src, dst_ref=dst, send_sem=send, recv_sem=recv, device_id=device, device_id_type=MESH
         )
-
-    rim_copies = [
-        remote(src.at[pl.ds(toks - RIM, RIM), :], rims.at[i], rim_send.at[i], rim_recv.at[i], (after, head))
-        for i, src in enumerate((q_hbm, k_hbm, v_hbm))
-    ]
-    for copy in rim_copies:
-        copy.start()
 
     row, col = iotas(toks)
     inclusive = row >= col
@@ -130,36 +136,68 @@
     loss = jnp.exp(last) - 1.0
     strength = 1.0 / (1.0 + jnp.exp(-beta_in[...]))
 
-    conved = []
     for load in loads[:3]:
         load.wait()
+    raws = (q_in, k_in, v_in)
+    for i in range(3):
+        ext[i, 0:RIM, :] = jnp.zeros((RIM, feat), F32)
+        ext[i, RIM : RIM + toks, :] = raws[i][...].astype(F32)
+    conved = [conv_silu(ext, taps_in, i, toks) for i in range(3)]
+
+    pl.semaphore_wait(barrier, len(greet))
+    rim_copies = [
+        remote(src.at[pl.ds(toks - RIM, RIM), :], rims.at[i], rim_send.at[i], rim_recv.at[i], (after, head))
+        for i, src in enumerate((q_hbm, k_hbm, v_hbm))
+    ]
+    for copy in rim_copies:
+        copy.start()
+
+    def head_parts(parts_of, h, rows):
+        cols = slice(h * HW, (h + 1) * HW)
+        q_h, k_h, v_h = (part[:, cols] for part in parts_of)
+        q_h = q_h * lax.rsqrt(jnp.sum(q_h * q_h, axis=-1, keepdims=True) + 1e-06)
+        k_h = k_h * lax.rsqrt(jnp.sum(k_h * k_h, axis=-1, keepdims=True) + 1e-06)
+        return k_h * grow[:rows, cols], k_h * shrink[:rows, cols], q_h * grow[:rows, cols], v_h
+
+    betas, firsts, lowers = [], [], []
+    for h in range(local_heads):
+        betas.append(jnp.transpose(jnp.broadcast_to(strength[h : h + 1, :], (HW, toks))))
+        firsts.append(head_parts(conved, h, toks))
+        lower = mm_full(firsts[h][0], jnp.transpose(firsts[h][1])) * betas[h]
+        lowers.append(jnp.where(strict & (col >= EDGE), lower, 0.0))
+    inverses = unit_lower_inverses(lowers, row, col)
+
     for copy in rim_copies:
         copy.wait_recv()
-    for i, inp in enumerate((q_in, k_in, v_in)):
+    for i in range(3):
         ext[i, 0:RIM, :] = jnp.where(seq > 0, rims[i].astype(F32), 0.0)
-        ext[i, RIM : RIM + toks, :] = inp[...].astype(F32)
-        total = jnp.zeros((toks, feat), F32)
-        for j in range(CONV):
-            first = RIM - (CONV - 1) + j
-            total = total + ext[i, first : first + toks, :] * taps_in[i, j : j + 1, :]
-        conved.append(total / (1.0 + jnp.exp(-total)))
-
-    queries, keys, values, lowers, scores, betas = [], [], [], [], [], []
+    edges = [conv_silu(ext, taps_in, i, EDGE) for i in range(3)]
+    queries, keys, scores, sides, corners = [], [], [], [], []
     for h in range(local_heads):
         cols = slice(h * HW, (h + 1) * HW)
-        q_h, k_h, v_h = (part[:, cols] for part in conved)
-        q_h = q_h * lax.rsqrt(jnp.sum(q_h * q_h, axis=-1, keepdims=True) + 1e-06)
-        k_h = k_h * lax.rsqrt(jnp.sum(k_h * k_h, axis=-1, keepdims=True) + 1e-06)
-        beta = jnp.transpose(jnp.broadcast_to(strength[h : h + 1, :], (HW, toks)))
-        key_pos, key_neg, query_pos = k_h * grow[:, cols], k_h * shrink[:, cols], q_h * grow[:, cols]
+        key_pos, key_neg, query_pos, v_h = (
+            jnp.concatenate([edge, part[EDGE:]], axis=0)
+            for edge, part in zip(head_parts(edges, h, EDGE), firsts[h])
+        )
         both = mm_full(jnp.concatenate([key_pos, query_pos], axis=0), jnp.transpose(key_neg))
-        lowers.append(jnp.where(strict, both[:toks] * beta, 0.0))
+        corners.append(jnp.where(strict & (col < EDGE), both[:toks] * betas[h], 0.0))
         scores.append(jnp.where(inclusive, both[toks:], 0.0))
         queries.append(query_pos * from_start[:, cols])
         keys.append(jnp.transpose(key_neg * to_end[:, cols]))
-        values.append(jnp.concatenate([key_pos * from_start[:, cols] * beta, v_h * beta], axis=1))
-    inverses = unit_lower_inverses(lowers, row, col)
-    solved = [mm_full(inv, rhs) for inv, rhs in zip(inverses, values)]
+        sides.append(jnp.concatenate([key_pos * from_start[:, cols] * betas[h], v_h * betas[h]], axis=1))
+    edge_sols = [side[:EDGE] for side in sides]
+    for j in range(EDGE - 1):
+        edge_sols = [
+            sol - corner[:EDGE, j : j + 1] * sol[j : j + 1, :] for sol, corner in zip(edge_sols, corners)
+        ]
+    below = [
+        mm_full(corner, jnp.concatenate([sol, jnp.zeros((toks - EDGE, 2 * HW), F32)], axis=0))
+        for corner, sol in zip(corners, edge_sols)
+    ]
+    solved = [
+        mm_full(inv, jnp.concatenate([sol, side[EDGE:] - low[EDGE:]], axis=0))
+        for inv, sol, side, low in zip(inverses, edge_sols, sides, below)
+    ]
     for h in range(local_heads):
         cols = slice(h * HW, (h + 1) * HW)
         outs = mm_full(jnp.concatenate([scores[h], keys[h]], axis=0), solved[h])
@@ -170,7 +208,7 @@
 
     def exchange(send_of, recv, mine, at, sends, recvs):
         out, arrive = [], []
-        for d in (1, 2, 3):
+        for d in (2, 1, 3):
             copy = remote(send_of((mine + d) % 4), recv.at[mine], sends.at[d - 1], recvs.at[d - 1], (at(d), head))
             copy.start()
             out.append(copy)
@@ -197,15 +235,29 @@
         before2 = jnp.where(a == n, run, before2)
         run = compose(e2_recv[n], run)
 
-    e3_send[...] = run.astype(BF16)
-    out3, arrive3 = exchange(lambda h: e3_send, e3_recv, x, at3, l3s, l3r)
-    for copy in arrive3:
-        copy.wait_recv()
-    state = e3_recv[0, :, HW:].astype(F32)
+    n3_send[...] = run[:, HW:].astype(BF16)
+    e3_send[...] = run[:, :HW].astype(BF16)
+    out3n = [remote(n3_send, n3_recv.at[x], l3s.at[d - 1], l3r.at[d - 1], (at3(d), head)) for d in (1, 2, 3)]
+    out3e = [remote(e3_send, e3_recv.at[x], l3s.at[d + 2], l3r.at[d + 2], (at3(d), head)) for d in (1, 2)]
+    came3n = [
+        remote(n3_send, n3_recv.at[(x + 4 - d) % 4], l3s.at[d - 1], l3r.at[d - 1], (at3(d), head)) for d in (1, 2, 3)
+    ]
+    came3e = [
+        remote(e3_send, e3_recv.at[(x + 4 - d) % 4], l3s.at[d + 2], l3r.at[d + 2], (at3(d), head)) for d in (1, 2)
+    ]
+    for d in (2, 1, 3):
+        pl.when(x + d < 4)(out3n[d - 1].start)
+    for d in (2, 1):
+        pl.when((x >= 1) & (x + d < 4))(out3e[d - 1].start)
+    for d in (1, 2, 3):
+        pl.when(x >= d)(came3n[d - 1].wait_recv)
+    for d in (1, 2):
+        pl.when(x >= d + 1)(came3e[d - 1].wait_recv)
+    state = n3_recv[0].astype(F32)
     entering = jnp.zeros_like(state)
     entering = jnp.where(x == 1, state, entering)
     for n in (1, 2):
-        state = state + mm_exact_left(e3_recv[n, :, :HW], state) + e3_recv[n, :, HW:].astype(F32)
+        state = state + mm_exact_left(e3_recv[n], state) + n3_recv[n].astype(F32)
         entering = jnp.where(x == n + 1, state, entering)
     entering = entering + mm_full(before2[:, :HW], entering) + before2[:, HW:]
     s4_send[0] = entering.astype(BF16)
@@ -230,34 +282,43 @@
     loads[7].wait()
     width = w_in.shape[1] // CHUNKS
     rows = toks // heads
-    sent, coming = [], []
+    core, place = head % 2, head // 2
+    pairs, spread, coming = [], [], []
     for c in range(CHUNKS):
         cols = slice(c * width, (c + 1) * width)
         partial = mm(normed, w_in[:, cols]).astype(BF16)
         for t in range(heads):
-            parts[t, :, cols] = partial[t * rows : (t + 1) * rows]
-        for d in range(1, heads):
-            to, source = (head + d) % heads, (head + heads - d) % heads
-            at = pl.ds(c * width, width)
-            copy = remote(
-                parts.at[to, :, at], landed.at[head, :, at], rss.at[c, d - 1], rsr.at[c, d - 1], (seq, to)
-            )
-            copy.start()
-            sent.append(copy)
-            coming.append(
-                remote(
-                    parts.at[to, :, at], landed.at[source, :, at], rss.at[c, d - 1], rsr.at[c, d - 1], (seq, to)
-                )
-            )
+            parts[t % 2, (t // 2) * rows : (t // 2 + 1) * rows, cols] = partial[t * rows : (t + 1) * rows]
+        copy = remote(parts.at[1 - core, :, cols], paired.at[:, cols], prs.at[c], prr.at[c], (seq, other))
+        copy.start()
+        pairs.append(copy)
     for c in range(CHUNKS):
         cols = slice(c * width, (c + 1) * width)
-        summed = parts[head, :, cols].astype(F32)
-        for d in range(1, heads):
-            coming[c * (heads - 1) + d - 1].wait_recv()
-            summed = summed + landed[(head + heads - d) % heads, :, cols].astype(F32)
-        o_ref[:, cols] = summed.astype(BF16)
-    for copy in rim_copies + out1 + out2 + out3 + out4 + sent:
+        pairs[c].wait_recv()
+        both = parts[core, :, cols].astype(F32) + paired[:, cols].astype(F32)
+        for t in range(4):
+            summed[t, :, cols] = both[t * rows : (t + 1) * rows].astype(BF16)
+        for d in (2, 1, 3):
+            to, source = (place + d) % 4, (place + 4 - d) % 4
+            ends = (rss.at[c, d - 1], rsr.at[c, d - 1], (seq, across(d)))
+            copy = remote(summed.at[to, :, cols], landed.at[place, :, cols], *ends)
+            copy.start()
+            spread.append(copy)
+            coming.append(remote(summed.at[to, :, cols], landed.at[source, :, cols], *ends))
+    for c in range(CHUNKS):
+        cols = slice(c * width, (c + 1) * width)
+        total = summed[place, :, cols].astype(F32)
+        for copy in coming[3 * c : 3 * c + 3]:
+            copy.wait_recv()
+        for d in (1, 2, 3):
+            total = total + landed[(place + d) % 4, :, cols].astype(F32)
+        o_ref[:, cols] = total.astype(BF16)
+    for copy in rim_copies + out1 + out2 + out4 + pairs + spread:
         copy.wait_send()
+    for d in (1, 2, 3):
+        pl.when(x + d < 4)(out3n[d - 1].wait_send)
+    for d in (1, 2):
+        pl.when((x >= 1) & (x + d < 4))(out3e[d - 1].wait_send)
 
 
 def body(q_raw, k_raw, v_raw, log_decay, beta_logit, conv_weight, norm_gain, out_weight):
@@ -278,27 +339,31 @@
         pltpu.VMEM((4, HW, 2 * HW), BF16),
         pltpu.VMEM((HW, 2 * HW), BF16),
         pltpu.VMEM((4, HW, 2 * HW), BF16),
-        pltpu.VMEM((HW, 2 * HW), BF16),
-        pltpu.VMEM((4, HW, 2 * HW), BF16),
+        pltpu.VMEM((HW, HW), BF16),
+        pltpu.VMEM((4, HW, HW), BF16),
+        pltpu.VMEM((HW, HW), BF16),
         pltpu.VMEM((4, HW, HW), BF16),
         pltpu.VMEM((4, HW, HW), BF16),
-        pltpu.VMEM((heads, toks // heads, width), BF16),
-        pltpu.VMEM((heads, toks // heads, width), BF16),
+        pltpu.VMEM((4, HW, HW), BF16),
+        pltpu.VMEM((2, toks // 2, width), BF16),
+        pltpu.VMEM((toks // 2, width), BF16),
+        pltpu.VMEM((4, toks // heads, width), BF16),
+        pltpu.VMEM((4, toks // heads, width), BF16),
         dma((len(operands),)), dma((3,)), dma((3,)),
-        dma((3,)), dma((3,)), dma((3,)), dma((3,)), dma((3,)), dma((3,)), dma((3,)), dma((3,)),
-        dma((CHUNKS, heads - 1)), dma((CHUNKS, heads - 1)),
+        dma((3,)), dma((3,)), dma((3,)), dma((3,)), dma((5,)), dma((5,)), dma((3,)), dma((3,)),
+        dma((CHUNKS,)), dma((CHUNKS,)), dma((CHUNKS, 3)), dma((CHUNKS, 3)),
     ]
     return pl.pallas_call(
         kernel,
         out_shape=jax.ShapeDtypeStruct((toks // heads, width), BF16),
-        in_specs=[pl.BlockSpec(memory_space=pl.ANY)] * len(operands),
+        in_specs=[pl.BlockSpec(memory_space=pltpu.HBM)] * len(operands),
         out_specs=pl.BlockSpec(memory_space=pltpu.VMEM),
         scratch_shapes=scratch,
         compiler_params=pltpu.CompilerParams(
             collective_id=0, has_side_effects=True, vmem_limit_bytes=48 * 2**20
         ),
         cost_estimate=pl.CostEstimate(flops=2 * 10**9, bytes_accessed=3 * 10**6, transcendentals=10**6),
-    )(*operands)
+    )(*[pltpu.with_memory_space_constraint(op, pltpu.HBM) for op in operands])
 
 
 def solution(mesh):

time: 71.6 us -> 60.5 us (0.84)
  the two profiles are of different devices: /device:TPU:1 before, /device:TPU:7 now
where the time goes in v2:
time: 60.5 us; the launch traced here: 60 us
  Pallas kernels  59.4 us (98%)
  local copies, waits for them, and re-layouts  0.64 us (1%)
    pallas_call x1, Pallas kernels, body(): pl.pallas_call(kernel, out_shape=jax.ShapeDtypeStruct((toks // heads, wid...  59.4 us

profile of v2, /device:TPU:7, one launch (start us, length us, event | category | flops | bytes accessed | tf_op | source)
XLA Modules:
  0.0 60.0 jit_solution(3906725631094276627)
XLA Ops:
  0.0 59.4 %shard_map.82 = bf16[16,2304]{1,0:T(8,128)(2,1)S(1)} custom-call(bf16[128,512]{1,0:T(8,128)(2,1)} %q_hbm.1, bf16[128,512]{1,0:T(8,128)(2,1)} %k_hbm.1, bf16[128,512]{1,0:T(8,128)(2,1)} %v_hbm.1, bf16[128,512]{1,0:T(8,128)(2,1)} %ld_hbm.1, f32[4,128]{1,0:T(4,128)} %beta_hbm.1, f32[3,4,512]{2,1,0:T(4,128)} %taps_hbm.1, f32[1,512]{1,0:T(1,128)} %bitcast.1, ...), custom_call_target="tpu_custom_call" | custom-call | flops 2000000000 | bytes 3000000 | tf_op jit(solution)/shard_map/pallas_call | solution.py:356
  59.4 0.6 %copy.10 = bf16[16,2304]{1,0:T(8,128)(2,1)} copy(bf16[16,2304]{1,0:T(8,128)(2,1)S(1)} %shard_map.82) | data formatting | bytes 147456

commit v3 on v2

--- a/solution.py
+++ b/solution.py
@@ -14,7 +14,7 @@
 CONV = 4
 RIM = 16
 EDGE = 8
-CHUNKS = 3
+CHUNKS = 1
 
 
 def halves(value):
@@ -120,6 +120,19 @@
             src_ref=src, dst_ref=dst, send_sem=send, recv_sem=recv, device_id=device, device_id_type=MESH
         )
 
+    def go(copies, when=None):
+        @pl.when(seq >= 0 if when is None else when)
+        def _():
+            for copy in copies:
+                copy.start()
+
+    pl.semaphore_wait(barrier, len(greet))
+    rim_copies = [
+        remote(src.at[pl.ds(toks - RIM, RIM), :], rims.at[i], rim_send.at[i], rim_recv.at[i], (after, head))
+        for i, src in enumerate((q_hbm, k_hbm, v_hbm))
+    ]
+    go(rim_copies)
+
     row, col = iotas(toks)
     inclusive = row >= col
     strict = row > col
@@ -144,13 +157,6 @@
         ext[i, RIM : RIM + toks, :] = raws[i][...].astype(F32)
     conved = [conv_silu(ext, taps_in, i, toks) for i in range(3)]
 
-    pl.semaphore_wait(barrier, len(greet))
-    rim_copies = [
-        remote(src.at[pl.ds(toks - RIM, RIM), :], rims.at[i], rim_send.at[i], rim_recv.at[i], (after, head))
-        for i, src in enumerate((q_hbm, k_hbm, v_hbm))
-    ]
-    for copy in rim_copies:
-        copy.start()
 
     def head_parts(parts_of, h, rows):
         cols = slice(h * HW, (h + 1) * HW)
@@ -165,10 +171,14 @@
         firsts.append(head_parts(conved, h, toks))
         lower = mm_full(firsts[h][0], jnp.transpose(firsts[h][1])) * betas[h]
         lowers.append(jnp.where(strict & (col >= EDGE), lower, 0.0))
-    inverses = unit_lower_inverses(lowers, row, col)
-
-    for copy in rim_copies:
-        copy.wait_recv()
+    for h, inv in enumerate(unit_lower_inverses(lowers, row, col)):
+        qeff[h] = inv
+
+    @pl.when(seq >= 0)
+    def _():
+        for copy in rim_copies:
+            copy.wait_recv()
+
     for i in range(3):
         ext[i, 0:RIM, :] = jnp.where(seq > 0, rims[i].astype(F32), 0.0)
     edges = [conv_silu(ext, taps_in, i, EDGE) for i in range(3)]
@@ -196,7 +206,7 @@
     ]
     solved = [
         mm_full(inv, jnp.concatenate([sol, side[EDGE:] - low[EDGE:]], axis=0))
-        for inv, sol, side, low in zip(inverses, edge_sols, sides, below)
+        for inv, sol, side, low in zip([qeff[h] for h in range(local_heads)], edge_sols, sides, below)
     ]
     for h in range(local_heads):
         cols = slice(h * HW, (h + 1) * HW)
@@ -209,11 +219,11 @@
     def exchange(send_of, recv, mine, at, sends, recvs):
         out, arrive = [], []
         for d in (2, 1, 3):
-            copy = remote(send_of((mine + d) % 4), recv.at[mine], sends.at[d - 1], recvs.at[d - 1], (at(d), head))
-            copy.start()
-            out.append(copy)
+            ends = (sends.at[d - 1], recvs.at[d - 1], (at(d), head))
+            out.append(remote(send_of((mine + d) % 4), recv.at[mine], *ends))
             slot = (mine + 4 - d) % 4
-            arrive.append(remote(send_of(slot), recv.at[slot], sends.at[d - 1], recvs.at[d - 1], (at(d), head)))
+            arrive.append(remote(send_of(slot), recv.at[slot], *ends))
+        go(out)
         return out, arrive
 
     out1, arrive1 = exchange(lambda h: e1_send.at[h], e1_recv, b, at1, l1s, l1r)
@@ -289,9 +299,8 @@
         partial = mm(normed, w_in[:, cols]).astype(BF16)
         for t in range(heads):
             parts[t % 2, (t // 2) * rows : (t // 2 + 1) * rows, cols] = partial[t * rows : (t + 1) * rows]
-        copy = remote(parts.at[1 - core, :, cols], paired.at[:, cols], prs.at[c], prr.at[c], (seq, other))
-        copy.start()
-        pairs.append(copy)
+        pairs.append(remote(parts.at[1 - core, :, cols], paired.at[:, cols], prs.at[c], prr.at[c], (seq, other)))
+        go(pairs[-1:])
     for c in range(CHUNKS):
         cols = slice(c * width, (c + 1) * width)
         pairs[c].wait_recv()
@@ -301,10 +310,9 @@
         for d in (2, 1, 3):
             to, source = (place + d) % 4, (place + 4 - d) % 4
             ends = (rss.at[c, d - 1], rsr.at[c, d - 1], (seq, across(d)))
-            copy = remote(summed.at[to, :, cols], landed.at[place, :, cols], *ends)
-            copy.start()
-            spread.append(copy)
+            spread.append(remote(summed.at[to, :, cols], landed.at[place, :, cols], *ends))
             coming.append(remote(summed.at[to, :, cols], landed.at[source, :, cols], *ends))
+        go(spread[-3:])
     for c in range(CHUNKS):
         cols = slice(c * width, (c + 1) * width)
         total = summed[place, :, cols].astype(F32)

time: 60.5 us -> 58 us (0.959)
  Pallas kernels: 59.4 us -> 57.3 us
    pallas_call x1, Pallas kernels: 59.4 us -> 57.3 us  [body(): pl.pallas_call(kernel, out_shape=jax.ShapeDtypeStruct((toks // heads, wid...]
where the time goes in v3:
time: 58 us; the launch traced here: 57.9 us
  Pallas kernels  57.3 us (99%)
  local copies, waits for them, and re-layouts  0.64 us (1%)
    pallas_call x1, Pallas kernels, body(): pl.pallas_call(kernel, out_shape=jax.ShapeDtypeStruct((toks // heads, wid...  57.3 us

profile of v3, /device:TPU:7, one launch (start us, length us, event | category | flops | bytes accessed | tf_op | source)
XLA Modules:
  0.0 57.9 jit_solution(16187241534994109591)
XLA Ops:
  0.0 57.3 %shard_map.82 = bf16[16,2304]{1,0:T(8,128)(2,1)S(1)} custom-call(bf16[128,512]{1,0:T(8,128)(2,1)} %q_hbm.1, bf16[128,512]{1,0:T(8,128)(2,1)} %k_hbm.1, bf16[128,512]{1,0:T(8,128)(2,1)} %v_hbm.1, bf16[128,512]{1,0:T(8,128)(2,1)} %ld_hbm.1, f32[4,128]{1,0:T(4,128)} %beta_hbm.1, f32[3,4,512]{2,1,0:T(4,128)} %taps_hbm.1, f32[1,512]{1,0:T(1,128)} %bitcast.1, ...), custom_call_target="tpu_custom_call" | custom-call | flops 2000000000 | bytes 3000000 | tf_op jit(solution)/shard_map/pallas_call | solution.py:364
  57.3 0.6 %copy.10 = bf16[16,2304]{1,0:T(8,128)(2,1)} copy(bf16[16,2304]{1,0:T(8,128)(2,1)S(1)} %shard_map.82) | data formatting | bytes 147456

commit v4 on v3

--- a/solution.py
+++ b/solution.py
@@ -235,7 +235,19 @@
         maps1.append(compose(e1_recv[n], maps1[-1]))
 
     e2_send[...] = maps1[3].astype(BF16)
-    out2, arrive2 = exchange(lambda h: e2_send, e2_recv, a, at2, l2s, l2r)
+    out2, arrive2 = [], []
+    for i in range(3):
+        target, source = i + (i + 4 - a) // 4, (a + i + 1) % 4
+        d, gap = (target + 4 - a) % 4, (a + 4 - source) % 4
+        out2.append(
+            remote(e2_send, e2_recv.at[a], l2s.at[d - 1], l2r.at[d - 1], (seq - 4 * a + 4 * target, head))
+        )
+        arrive2.append(
+            remote(e2_send, e2_recv.at[source], l2s.at[gap - 1], l2r.at[gap - 1], (seq - 4 * a + 4 * source, head))
+        )
+    go(out2[:1])
+    go(out2[1:2])
+    go(out2[2:])
     e2_recv[a] = e2_send[...]
     for copy in arrive2:
         copy.wait_recv()

time: 58 us -> 57 us (0.983)
  Pallas kernels: 57.3 us -> 56.2 us
    pallas_call x1, Pallas kernels: 57.3 us -> 56.2 us  [body(): pl.pallas_call(kernel, out_shape=jax.ShapeDtypeStruct((toks // heads, wid...]
where the time goes in v4:
time: 57 us; the launch traced here: 56.8 us
  Pallas kernels  56.2 us (99%)
  local copies, waits for them, and re-layouts  0.64 us (1%)
    pallas_call x1, Pallas kernels, body(): pl.pallas_call(kernel, out_shape=jax.ShapeDtypeStruct((toks // heads, wid...  56.2 us

profile of v4, /device:TPU:7, one launch (start us, length us, event | category | flops | bytes accessed | tf_op | source)
XLA Modules:
  0.0 56.8 jit_solution(3319791861682066826)
XLA Ops:
  0.0 56.2 %shard_map.82 = bf16[16,2304]{1,0:T(8,128)(2,1)S(1)} custom-call(bf16[128,512]{1,0:T(8,128)(2,1)} %q_hbm.1, bf16[128,512]{1,0:T(8,128)(2,1)} %k_hbm.1, bf16[128,512]{1,0:T(8,128)(2,1)} %v_hbm.1, bf16[128,512]{1,0:T(8,128)(2,1)} %ld_hbm.1, f32[4,128]{1,0:T(4,128)} %beta_hbm.1, f32[3,4,512]{2,1,0:T(4,128)} %taps_hbm.1, f32[1,512]{1,0:T(1,128)} %bitcast.1, ...), custom_call_target="tpu_custom_call" | custom-call | flops 2000000000 | bytes 3000000 | tf_op jit(solution)/shard_map/pallas_call | solution.py:376
  56.2 0.6 %copy.10 = bf16[16,2304]{1,0:T(8,128)(2,1)} copy(bf16[16,2304]{1,0:T(8,128)(2,1)S(1)} %shard_map.82) | data formatting | bytes 147456
